TPU v7x, 32 devices: a whole 2x2x4 slice. The times are simulated.
32 devices in a mesh: section: 2 (over y), ctx: 16 (over z, x, core), tp: 1.
Axes of the slice: x: 2, y: 2, z: 4, core: 2. Of those that a mesh axis runs over, the one named last changes fastest.
Arguments:
- query_heads: bfloat16 [2, 2, 2048, 6144], P('section', None, 'ctx', 'tp'), may hold values from -8 to 8
- keys_values: bfloat16 [2, 2048, 2, 1024], P('section', 'ctx', None, 'tp'), may hold values from -12 to 12
- grad_output: bfloat16 [2, 2, 2048, 6144], P('section', None, 'ctx', 'tp'), may hold values from -6 to 6
- norm_gain: float32 [2, 2, 6144], P('section', None, 'tp'), may hold values from 0.1 to 1.9
- turn_ids: int32 [2048], P('ctx'), may hold values from 0 to 63, never falling along the last dimension, each value on 1 to 64 neighbouring positions
Outputs:
- normed_out: bfloat16 [2, 2, 2048, 6144], P('section', None, 'ctx', 'tp')
- query_grad: bfloat16 [2, 2, 2048, 6144], P('section', None, 'ctx', 'tp')
- kv_grad: float32 [2, 2048, 2, 1024], P('section', 'ctx', None, 'tp')
Inputs may be any that keep to these rules, and one draw needn't show every extreme that they name: `turn_ids`: turn numbers never fall along the dialogue; a turn holds 1 to 64 positions and one holds exactly 64; every turn number occurs.
All inputs are finite; a program needn't handle non-finite values.
Results may differ from a plain program's by a relative error of at most 0.015.
Values may be sent and summed in bfloat16 or wider, within the bound.
A program may use at most 128 MiB of HBM per device.

v0:
```python
import jax
import jax.numpy as jnp
from jax import lax
from jax.sharding import PartitionSpec as P

HD = 128
KVH = 8
GROUP = 6


neg_big = -1e30
eps_norm = 1e-06


def passed_along(block, axis, distance):
    devices = range(lax.axis_size(axis))
    route = [((i - distance) % len(devices), i) for i in devices]
    return lax.ppermute(block, axis, route)


def visible_mask(query_pos, query_seg, key_pos, key_seg):
    return (key_pos[None, :] <= query_pos[:, None]) | (key_seg[None, :] == query_seg[:, None])


def block_terms(queries, kv_rows, scaling):
    row_count = kv_rows.shape[0]
    head_count = queries.shape[1]
    key_rows = kv_rows[:, 0].reshape(row_count, head_count, HD)
    value_rows = kv_rows[:, 1].reshape(row_count, head_count, HD)
    scores = (
        jnp.einsum("qhgd,khd->hgqk", queries, key_rows, preferred_element_type=jnp.float32)
        * scaling
    )
    return (scores, key_rows, value_rows)


def run_layer(queries_flat, gathered, key_seg, query_pos, query_seg, gain_vector, cotangent_flat):
    tokens_here = queries_flat.shape[0]
    head_count = gathered.shape[2] // HD
    queries = queries_flat.reshape(tokens_here, head_count, GROUP, HD)
    scaling = HD ** (-0.5)
    seq_len = gathered.shape[0]
    span_rows = min(512, seq_len)
    blocks = seq_len // span_rows

    def block_view(number):
        offset = number * span_rows
        kv_rows = lax.dynamic_slice_in_dim(gathered, offset, span_rows, 0)
        key_pos = offset + jnp.arange(span_rows, dtype=jnp.int32)
        visible = visible_mask(
            query_pos, query_seg, key_pos, lax.dynamic_slice_in_dim(key_seg, offset, span_rows, 0)
        )
        scores, key_rows, value_rows = block_terms(queries, kv_rows, scaling)
        return (scores, key_rows, value_rows, visible)

    def forward_step(running, number):
        run_max, run_sum, accumulated = running
        scores, key_rows, value_rows, visible = block_view(number)
        new_max = jnp.maximum(run_max, jnp.max(jnp.where(visible, scores, neg_big), axis=-1))
        weights = jnp.where(visible, jnp.exp(scores - new_max[..., None]), 0.0)
        factor = jnp.exp(run_max - new_max)
        run_sum = run_sum * factor + jnp.sum(weights, axis=-1)
        update = jnp.einsum(
            "hgqk,khd->qhgd",
            weights.astype(jnp.bfloat16),
            value_rows,
            preferred_element_type=jnp.float32,
        )
        accumulated = accumulated * jnp.transpose(factor, (2, 0, 1))[..., None] + update
        return ((new_max, run_sum, accumulated), None)

    start_state = (
        jnp.full((head_count, GROUP, tokens_here), neg_big, jnp.float32),
        jnp.zeros((head_count, GROUP, tokens_here), jnp.float32),
        jnp.zeros((tokens_here, head_count, GROUP, HD), jnp.float32),
    )
    (row_max, row_sum, accumulated), unused = lax.scan(
        forward_step, start_state, jnp.arange(blocks, dtype=jnp.int32)
    )
    output = accumulated / jnp.transpose(row_sum, (2, 0, 1))[..., None]
    gain_grid = gain_vector.reshape(head_count, GROUP, HD)
    scaled = (
        cotangent_flat.reshape(tokens_here, head_count, GROUP, HD).astype(jnp.float32) * gain_grid
    )
    local_sq = jnp.sum(output * output, axis=(1, 2, 3))
    local_dot = jnp.sum(scaled * output, axis=(1, 2, 3))
    total_sq, total_dot = lax.psum((local_sq, local_dot), "tp")
    features = KVH * GROUP * HD
    inverse = lax.rsqrt(total_sq / features + eps_norm)
    normed = (output * inverse[:, None, None, None] * gain_grid).astype(jnp.bfloat16)
    center = total_dot / features
    out_grad = (
        inverse[:, None, None, None]
        * (scaled - output * (inverse * inverse * center)[:, None, None, None])
    ).astype(jnp.bfloat16)
    row_dot = jnp.transpose(jnp.sum(out_grad.astype(jnp.float32) * output, axis=-1), (1, 2, 0))

    def backward_step(grad_q, number):
        scores, key_rows, value_rows, visible = block_view(number)
        chances = jnp.where(visible, jnp.exp(scores - row_max[..., None]), 0.0) / row_sum[..., None]
        value_grad = jnp.einsum(
            "hgqk,qhgd->khd",
            chances.astype(jnp.bfloat16),
            out_grad,
            preferred_element_type=jnp.float32,
        )
        prob_grad = jnp.einsum(
            "qhgd,khd->hgqk", out_grad, value_rows, preferred_element_type=jnp.float32
        )
        score_grad = (chances * (prob_grad - row_dot[..., None])).astype(jnp.bfloat16)
        grad_q = (
            grad_q
            + jnp.einsum("hgqk,khd->qhgd", score_grad, key_rows, preferred_element_type=jnp.float32)
            * scaling
        )
        key_grad = (
            jnp.einsum("hgqk,qhgd->khd", score_grad, queries, preferred_element_type=jnp.float32)
            * scaling
        )
        return (grad_q, jnp.stack([key_grad, value_grad], axis=1))

    grad_q, pieces = lax.scan(
        backward_step,
        jnp.zeros((tokens_here, head_count, GROUP, HD), jnp.float32),
        jnp.arange(blocks, dtype=jnp.int32),
    )
    kv_partial = pieces.reshape(seq_len, 2, head_count * HD)
    return (
        normed.reshape(tokens_here, -1),
        grad_q.reshape(tokens_here, -1).astype(jnp.bfloat16),
        kv_partial,
    )


def on_device(query_heads, keys_values, grad_output, norm_gain, turn_ids):
    tokens_here = turn_ids.shape[0]
    query_pos = lax.axis_index("ctx") * tokens_here + jnp.arange(tokens_here, dtype=jnp.int32)
    own_rows = keys_values[0]
    earlier = passed_along(own_rows, "section", 1)
    own_full, key_seg = (
        lax.all_gather(own_rows, "ctx", axis=0, tiled=True),
        lax.all_gather(turn_ids, "ctx", axis=0, tiled=True),
    )
    earlier_full = lax.all_gather(earlier, "ctx", axis=0, tiled=True)
    producer = run_layer(
        query_heads[0, 0],
        own_full,
        key_seg,
        query_pos,
        turn_ids,
        norm_gain[0, 0],
        grad_output[0, 0],
    )
    consumer = run_layer(
        query_heads[0, 1],
        earlier_full,
        key_seg,
        query_pos,
        turn_ids,
        norm_gain[0, 1],
        grad_output[0, 1],
    )
    normed = jnp.stack([producer[0], consumer[0]])[None]
    grad_q = jnp.stack([producer[1], consumer[1]])[None]
    own_sum = lax.psum_scatter(
        producer[2].astype(jnp.bfloat16), "ctx", scatter_dimension=0, tiled=True
    ).astype(jnp.float32)
    their_sum = lax.psum_scatter(
        consumer[2].astype(jnp.bfloat16), "ctx", scatter_dimension=0, tiled=True
    ).astype(jnp.float32)
    kv_grad = own_sum + passed_along(their_sum.astype(jnp.bfloat16), "section", -1).astype(
        their_sum.dtype
    )
    return (normed, grad_q, kv_grad[None])


def solution(mesh):
    in_specs = (
        P("section", None, "ctx", "tp"),
        P("section", "ctx", None, "tp"),
        P("section", None, "ctx", "tp"),
        P("section", None, "tp"),
        P("ctx"),
    )
    out_specs = (
        P("section", None, "ctx", "tp"),
        P("section", None, "ctx", "tp"),
        P("section", "ctx", None, "tp"),
    )
    return jax.shard_map(
        on_device, mesh=mesh, in_specs=in_specs, out_specs=out_specs, check_vma=False
    )
```

profile of v0, /device:TPU:0, one launch (start us, length us, event | category | flops | bytes accessed | tf_op | source)
XLA Modules:
  0.0 920.2 jit_solution(7050081665072567334)
XLA Ops:
  34.6 21.6 %all-gather.1 = s32[16,1,128]{2,1,0:T(1,128)S(1)} all-gather(s32[1,1,128]{2,1,0:T(1,128)S(1)} %bitcast.364), channel_id=1, replica_groups=mesh['section'=2,'ctx'=16,'tp'=1] {'ctx'}, dimensions={0}, use_global_device_ids=true | all-gather | bytes 8704 | tf_op jit(solution)/shard_map/all_gather | solution.py:142
  56.4 35.1 %all-gather.7.cloned.1.call-done = bf16[1,2048,2,1024]{1,3,2,0:T(8,128)(2,1)} async-done(((bf16[1,128,2,1024]{1,3,2,0:T(8,128)(2,1)}), bf16[1,2048,2,1024]{1,3,2,0:T(8,128)(2,1)}) %all-gather.7.cloned.1.call-update) | async-done | bytes 8388624 | tf_op jit(solution)/shard_map/all_gather | solution.py:141
  91.6 98.4 %while.56 = (s32[]{:T(128)}, f32[8,6,128]{2,1,0:T(8,128)S(1)}, f32[8,6,128]{2,1,0:T(8,128)S(1)}, f32[128,8,6,128]{0,3,2,1:T(8,128)}, s32[4]{0:T(128)S(1)}, /*ind...) while((s32[]{:T(128)}, f32[8,6,128]{2,1,0:T(8,128)S(1)}, ...), condition=%wide.region_3.4_spmd.clone, body=%wide.region_0.3_spmd.clone.sunk | while | flops 1647809152 | bytes 109195048 | solution.py:77
  95.9 6.8 fusion.154
  102.7 9.5 %bitcast_add_fusion.8 = f32[128,8,6,128]{0,3,2,1:T(8,128)} fusion(f32[128,8,6,128]{0,3,2,1:T(8,128)} %get-tuple-element.1042, bf16[512,8,128,1]{0,2,3,1:T(8,128)(2,1)} %bitcast.344, f32[8,512,128,6]{2,1,3,0:T(8,128)} %get-tuple-element.930, f32[8,6,128]{2,1,0:T(8,128)S(1)} %get-tuple-element.1055, pred[128,512]{0,1:T(8,128)(4,1)S(1)} %compare_or_fusion.8, ...), kind=kOutput, calls=%fused_computation.16.clone.1 | convolution fusion | flops 820248576 | bytes 20037632 | tf_op jit(solution)/shard_map/while/body/eval_jaxpr/hgqk,khd->qhgd/dot_general | solution.py:63
  126.1 11.5 %bitcast_add_fusion.8 = f32[128,8,6,128]{0,3,2,1:T(8,128)} fusion(f32[128,8,6,128]{0,3,2,1:T(8,128)} %get-tuple-element.1042, bf16[512,8,128,1]{0,2,3,1:T(8,128)(2,1)} %bitcast.344, f32[8,512,128,6]{2,1,3,0:T(8,128)} %get-tuple-element.930, f32[8,6,128]{2,1,0:T(8,128)S(1)} %get-tuple-element.1055, pred[128,512]{0,1:T(8,128)(4,1)S(1)} %compare_or_fusion.8, ...), kind=kOutput, calls=%fused_computation.16.clone.1 | convolution fusion | flops 820248576 | bytes 20037632 | tf_op jit(solution)/shard_map/while/body/eval_jaxpr/hgqk,khd->qhgd/dot_general | solution.py:63
  151.6 10.8 %bitcast_add_fusion.8 = f32[128,8,6,128]{0,3,2,1:T(8,128)} fusion(f32[128,8,6,128]{0,3,2,1:T(8,128)} %get-tuple-element.1042, bf16[512,8,128,1]{0,2,3,1:T(8,128)(2,1)} %bitcast.344, f32[8,512,128,6]{2,1,3,0:T(8,128)} %get-tuple-element.930, f32[8,6,128]{2,1,0:T(8,128)S(1)} %get-tuple-element.1055, pred[128,512]{0,1:T(8,128)(4,1)S(1)} %compare_or_fusion.8, ...), kind=kOutput, calls=%fused_computation.16.clone.1 | convolution fusion | flops 820248576 | bytes 20037632 | tf_op jit(solution)/shard_map/while/body/eval_jaxpr/hgqk,khd->qhgd/dot_general | solution.py:63
  176.7 10.4 %bitcast_add_fusion.8 = f32[128,8,6,128]{0,3,2,1:T(8,128)} fusion(f32[128,8,6,128]{0,3,2,1:T(8,128)} %get-tuple-element.1042, bf16[512,8,128,1]{0,2,3,1:T(8,128)(2,1)} %bitcast.344, f32[8,512,128,6]{2,1,3,0:T(8,128)} %get-tuple-element.930, f32[8,6,128]{2,1,0:T(8,128)S(1)} %get-tuple-element.1055, pred[128,512]{0,1:T(8,128)(4,1)S(1)} %compare_or_fusion.8, ...), kind=kOutput, calls=%fused_computation.16.clone.1 | convolution fusion | flops 820248576 | bytes 20037632 | tf_op jit(solution)/shard_map/while/body/eval_jaxpr/hgqk,khd->qhgd/dot_general | solution.py:63
  204.5 118.5 %while.58 = (s32[]{:T(128)}, f32[128,8,6,128]{0,3,2,1:T(8,128)S(1)}, bf16[4,512,2,8,128]{4,1,3,2,0:T(8,128)(2,1)}, s32[4]{0:T(128)S(1)}, bf16[2048,2,1024]{0,2,1...) while((s32[]{:T(128)}, ...), condition=%wide.region_13.14_spmd.clone, body=%wide.region_12.13_spmd.clone.sunk | while | flops 4059496960 | bytes 99832160 | solution.py:122
  323.0 13.2 %copy.72 = bf16[4,512,2,8,128]{4,3,2,1,0:T(8,128)(2,1)} copy(bf16[4,512,2,8,128]{4,1,3,2,0:T(8,128)(2,1)} %get-tuple-element.255) | data formatting | bytes 16777216 | tf_op jit(solution)/shard_map/convert_element_type | solution.py:166
  336.2 12.6 %convert_element_type.109 = bf16[2048,2,1024]{2,1,0:T(2,128)(2,1)} reshape(bf16[4,512,2,8,128]{4,3,2,1,0:T(8,128)(2,1)} %copy.72) | data formatting | bytes 16777216 | tf_op jit(solution)/shard_map/convert_element_type | solution.py:166
  348.8 91.4 %while.57 = (s32[]{:T(128)}, f32[8,6,128]{2,1,0:T(8,128)S(1)}, f32[8,6,128]{2,1,0:T(8,128)S(1)}, f32[128,8,6,128]{0,3,2,1:T(8,128)}, s32[4]{0:T(128)S(1)}, /*ind...) while((s32[]{:T(128)}, f32[8,6,128]{2,1,0:T(8,128)S(1)}, ...), condition=%wide.region_8.9_spmd.clone, body=%wide.region_5.0_spmd.clone.sunk | while | flops 1647809152 | bytes 109195048 | solution.py:77
  359.0 9.2 bitcast_add_fusion.9
  374.4 6.7 fusion.162
  381.2 10.1 %bitcast_add_fusion.9 = f32[128,8,6,128]{0,3,2,1:T(8,128)} fusion(f32[128,8,6,128]{0,3,2,1:T(8,128)} %get-tuple-element.997, bf16[512,8,128,1]{0,2,3,1:T(8,128)(2,1)S(1)} %bitcast.345, f32[8,512,128,6]{2,1,3,0:T(8,128)} %get-tuple-element.946, f32[8,6,128]{2,1,0:T(8,128)S(1)} %get-tuple-element.1010, pred[128,512]{0,1:T(8,128)(4,1)S(1)} %compare_or_fusion.9, ...), kind=kOutput, calls=%fused_computation.42.clone.1 | convolution fusion | flops 820248576 | bytes 20037632 | tf_op jit(solution)/shard_map/while/body/eval_jaxpr/hgqk,khd->qhgd/dot_general | solution.py:63
  397.5 6.7 fusion.162
  404.2 10.1 %bitcast_add_fusion.9 = f32[128,8,6,128]{0,3,2,1:T(8,128)} fusion(f32[128,8,6,128]{0,3,2,1:T(8,128)} %get-tuple-element.997, bf16[512,8,128,1]{0,2,3,1:T(8,128)(2,1)S(1)} %bitcast.345, f32[8,512,128,6]{2,1,3,0:T(8,128)} %get-tuple-element.946, f32[8,6,128]{2,1,0:T(8,128)S(1)} %get-tuple-element.1010, pred[128,512]{0,1:T(8,128)(4,1)S(1)} %compare_or_fusion.9, ...), kind=kOutput, calls=%fused_computation.42.clone.1 | convolution fusion | flops 820248576 | bytes 20037632 | tf_op jit(solution)/shard_map/while/body/eval_jaxpr/hgqk,khd->qhgd/dot_general | solution.py:63
  420.5 6.7 fusion.162
  427.2 10.1 %bitcast_add_fusion.9 = f32[128,8,6,128]{0,3,2,1:T(8,128)} fusion(f32[128,8,6,128]{0,3,2,1:T(8,128)} %get-tuple-element.997, bf16[512,8,128,1]{0,2,3,1:T(8,128)(2,1)S(1)} %bitcast.345, f32[8,512,128,6]{2,1,3,0:T(8,128)} %get-tuple-element.946, f32[8,6,128]{2,1,0:T(8,128)S(1)} %get-tuple-element.1010, pred[128,512]{0,1:T(8,128)(4,1)S(1)} %compare_or_fusion.9, ...), kind=kOutput, calls=%fused_computation.42.clone.1 | convolution fusion | flops 820248576 | bytes 20037632 | tf_op jit(solution)/shard_map/while/body/eval_jaxpr/hgqk,khd->qhgd/dot_general | solution.py:63
  453.6 118.6 %while.59 = (s32[]{:T(128)}, f32[128,8,6,128]{0,3,2,1:T(8,128)S(1)}, bf16[4,512,2,8,128]{4,1,3,2,0:T(8,128)(2,1)}, s32[4]{0:T(128)S(1)}, bf16[2048,2,1024]{0,2,1...) while((s32[]{:T(128)}, ...), condition=%wide.region_17.18_spmd.clone, body=%wide.region_16.17_spmd.clone.sunk | while | flops 4059496960 | bytes 99832160 | solution.py:122
  572.2 12.1 %copy.73 = bf16[4,512,2,8,128]{4,3,2,1,0:T(8,128)(2,1)} copy(bf16[4,512,2,8,128]{4,1,3,2,0:T(8,128)(2,1)} %get-tuple-element.256) | data formatting | bytes 16777216 | tf_op jit(solution)/shard_map/convert_element_type | solution.py:169
  584.3 12.6 %convert_element_type.112 = bf16[2048,2,1024]{2,1,0:T(2,128)(2,1)} reshape(bf16[4,512,2,8,128]{4,3,2,1,0:T(8,128)(2,1)} %copy.73) | data formatting | bytes 16777216 | tf_op jit(solution)/shard_map/convert_element_type | solution.py:169
  604.4 289.8 %all-reduce.5.cloned.1.call-done = (bf16[2048,2,1024]{2,1,0:T(2,128)(2,1)}, bf16[2048,2,1024]{2,1,0:T(2,128)(2,1)}) async-done(((bf16[2048,2,1024]{2,1,0:T(2,128)(2,1)}, bf16[2048,2,1024]{2,1,0:T(2,128)(2,1)}), (bf16[2048,2,1024]{2,1,0:T(2,128)(2,1)}, bf16[2048,2,1024]{2,1,0:T(2,128)(2,1)})) %all-reduce.5.cloned.1.call-update) | async-done | bytes 16777232
  902.8 7.8 collective-permute-done.1
  (339 shorter events, 379.4 us)
Async XLA Ops:
  7.2 84.4 %all-gather.7.cloned.1.call-start = ((), (), s32[]{:S(2)}) async-start(), calls=%async_computation.1 | async-start | bytes 8912896 | tf_op jit(solution)/shard_map/all_gather | solution.py:141
  9.3 339.6 %all-gather.5.cloned.1.call-start = ((), (), s32[]{:S(2)}) async-start(), calls=%async_computation | async-start | bytes 8912896 | tf_op jit(solution)/shard_map/all_gather | solution.py:144
  9.3 6.9 copy-start.17
  9.3 46.9 %collective-permute-start = (bf16[128,2,1024]{0,2,1:T(8,128)(2,1)}, bf16[128,2,1024]{0,2,1:T(8,128)(2,1)}, u32[]{:S(2)}, u32[]{:S(2)}) collective-permute-start(bf16[128,2,1024]{0,2,1:T(8,128)(2,1)} %bitcast.356), channel_id=1, source_target_pairs={{16,0},{0,16},{17,1},{1,17},{18,2},{2,18},{19,3},{3,19},{20,4},{4,... | collective-permute-start | bytes 1572872 | tf_op jit(solution)/shard_map/ppermute | solution.py:18
  56.2 838.0 %all-reduce.5.cloned.1.call-start = ((), (), s32[]{:S(2)}) async-start(), calls=%async_computation.2 | async-start | bytes 33554432
  102.7 9.5 %copy-start = (f32[8,512,128,6]{2,1,3,0:T(8,128)S(1)}, f32[8,512,128,6]{2,1,3,0:T(8,128)}, u32[]{:S(2)}) copy-start(f32[8,512,128,6]{2,1,3,0:T(8,128)} %get-tuple-element.930) | copy-start | bytes 37748740 | tf_op jit(solution)/shard_map/while
  126.1 11.5 %copy-start = (f32[8,512,128,6]{2,1,3,0:T(8,128)S(1)}, f32[8,512,128,6]{2,1,3,0:T(8,128)}, u32[]{:S(2)}) copy-start(f32[8,512,128,6]{2,1,3,0:T(8,128)} %get-tuple-element.930) | copy-start | bytes 37748740 | tf_op jit(solution)/shard_map/while
  151.5 10.8 %copy-start = (f32[8,512,128,6]{2,1,3,0:T(8,128)S(1)}, f32[8,512,128,6]{2,1,3,0:T(8,128)}, u32[]{:S(2)}) copy-start(f32[8,512,128,6]{2,1,3,0:T(8,128)} %get-tuple-element.930) | copy-start | bytes 37748740 | tf_op jit(solution)/shard_map/while
  176.6 10.4 %copy-start = (f32[8,512,128,6]{2,1,3,0:T(8,128)S(1)}, f32[8,512,128,6]{2,1,3,0:T(8,128)}, u32[]{:S(2)}) copy-start(f32[8,512,128,6]{2,1,3,0:T(8,128)} %get-tuple-element.930) | copy-start | bytes 37748740 | tf_op jit(solution)/shard_map/while
  219.0 6.1 copy-start.5
  248.5 6.1 copy-start.5
  278.0 6.1 copy-start.5
  307.6 6.1 copy-start.5
  323.0 13.3 %copy-start.3 = (f32[128,8,6,128]{0,3,2,1:T(8,128)}, f32[128,8,6,128]{0,3,2,1:T(8,128)S(1)}, u32[]{:S(2)}) copy-start(f32[128,8,6,128]{0,3,2,1:T(8,128)S(1)} %get-tuple-element.252) | copy-start | bytes 9437188
  336.2 12.6 %copy-start.16 = (f32[8,6,128]{2,1,0:T(8,128)S(1)}, f32[8,6,128]{2,1,0:T(8,128)}, u32[]{:S(2)}) copy-start(f32[8,6,128]{2,1,0:T(8,128)} %custom-call.3) | copy-start | bytes 73732
  336.2 12.6 %copy-start.18 = (f32[8,6,128]{2,1,0:T(8,128)S(1)}, f32[8,6,128]{2,1,0:T(8,128)}, u32[]{:S(2)}) copy-start(f32[8,6,128]{2,1,0:T(8,128)} %custom-call.4) | copy-start | bytes 73732
  348.8 91.5 %copy-start.19 = (f32[8,6,128]{2,1,0:T(8,128)S(1)}, f32[8,6,128]{2,1,0:T(8,128)}, u32[]{:S(2)}) copy-start(f32[8,6,128]{2,1,0:T(8,128)} %mul.235) | copy-start | bytes 73732
  359.0 9.2 copy-start.1
  381.1 10.1 %copy-start.1 = (f32[8,512,128,6]{2,1,3,0:T(8,128)S(1)}, f32[8,512,128,6]{2,1,3,0:T(8,128)}, u32[]{:S(2)}) copy-start(f32[8,512,128,6]{2,1,3,0:T(8,128)} %get-tuple-element.946) | copy-start | bytes 37748740 | tf_op jit(solution)/shard_map/while
  404.2 10.1 %copy-start.1 = (f32[8,512,128,6]{2,1,3,0:T(8,128)S(1)}, f32[8,512,128,6]{2,1,3,0:T(8,128)}, u32[]{:S(2)}) copy-start(f32[8,512,128,6]{2,1,3,0:T(8,128)} %get-tuple-element.946) | copy-start | bytes 37748740 | tf_op jit(solution)/shard_map/while
  427.2 10.1 %copy-start.1 = (f32[8,512,128,6]{2,1,3,0:T(8,128)S(1)}, f32[8,512,128,6]{2,1,3,0:T(8,128)}, u32[]{:S(2)}) copy-start(f32[8,512,128,6]{2,1,3,0:T(8,128)} %get-tuple-element.946) | copy-start | bytes 37748740 | tf_op jit(solution)/shard_map/while
  467.9 6.1 copy-start.4
  527.0 6.1 copy-start.4
  896.4 14.3 %collective-permute-start.1 = (bf16[128,2,1024]{2,1,0:T(2,128)(2,1)}, bf16[128,2,1024]{2,1,0:T(2,128)(2,1)}, u32[]{:S(2)}, u32[]{:S(2)}) collective-permute-start(bf16[128,2,1024]{2,1,0:T(2,128)(2,1)} %constant_dynamic-slice_fusion.8), channel_id=1, source_target_pairs={{16,0},{0,16},{17,1},{1,17},{18,2},{2,18},{19,3},{3,19},{20,4},{4,... | collective-permute-start | bytes 1572872 | tf_op jit(solution)/shard_map/ppermute | solution.py:18
  (34 other events, 115.9 us)
Sparse Core Ops, SparseCore 0:
  10.7 80.7 all-gather.6
  93.7 76.2 all-gather.4
  597.0 297.1 all-reduce.4
where the time goes:
time: 925 us; the launch traced here: 920 us
  waiting for transfers between devices  333 us (36%)
  matrix products  314 us (34%)
  local copies, waits for them, and re-layouts  151 us (16%)
  other arithmetic  67.9 us (7%)
  blocking collectives  21.6 us (2%)
  between operations  14.9 us (2%)
  loops' own time  12.5 us (1%)
    unnamed x4, waiting for transfers between devices  290 us
    dot_general x8, matrix products, forward_step(): jnp.einsum('hgqk,khd->qhgd', weights.astype(jnp.bfloat16), value_rows, pr...  81.6 us
    dot_general x16, matrix products, block_terms(): jnp.einsum('qhgd,khd->hgqk', queries, key_rows, preferred_element_type=jn...  79.2 us
    dot_general x8, matrix products, backward_step(): jnp.einsum('qhgd,khd->hgqk', out_grad, value_rows, preferred_element_type...  52.2 us
    dot_general x8, matrix products, backward_step(): jnp.einsum('hgqk,qhgd->khd', score_grad, queries, preferred_element_type=...  48.9 us
    slice x16, local copies, waits for them, and re-layouts, block_terms(): value_rows = kv_rows[:, 1].reshape(row_count, head_count, HD)  40.6 us
    dot_general x8, matrix products, backward_step(): jnp.einsum('hgqk,khd->qhgd', score_grad, key_rows, preferred_element_type...  38 us
    all_gather x1, waiting for transfers between devices, on_device(): lax.all_gather(own_rows, 'ctx', axis=0, tiled=True)  35.1 us
  transfers between devices with their start and end apart: 5, of which 3 were waited for; matrix products, arithmetic and copies ran while one was open for 31% of the time, Pallas kernels for 0%

commit v1 on v0

--- a/solution.py
+++ b/solution.py
@@ -1,6 +1,8 @@
 import jax
 import jax.numpy as jnp
 from jax import lax
+from jax.experimental import pallas as pl
+from jax.experimental.pallas import tpu as pltpu
 from jax.sharding import PartitionSpec as P
 
 HD = 128
@@ -10,6 +12,16 @@
 
 neg_big = -1e30
 eps_norm = 1e-06
+LOG2E = 1.4426950408889634
+SPAN = 512
+
+
+def dot_nn(a, b):
+    return jnp.dot(a, b, preferred_element_type=jnp.float32)
+
+
+def dot_nt(a, b):
+    return lax.dot_general(a, b, (((1,), (1,)), ((), ())), preferred_element_type=jnp.float32)
 
 
 def passed_along(block, axis, distance):
@@ -174,6 +186,205 @@
     return (normed, grad_q, kv_grad[None])
 
 
+def layer_kernel(
+    bounds, q_ref, k_ref, v_ref, g_ref, gain_ref, limit_ref,
+    normed_ref, dq_ref, dk_ref, dv_ref,
+    weights, scores, outs, recip, q_t, stack, grad_t, total, dots,
+):
+    phase, head = pl.program_id(0), pl.program_id(1)
+    seq_len = k_ref.shape[0]
+    rows = q_ref.shape[0]
+    wide = GROUP * rows
+    span = scores.shape[1]
+    blocks = seq_len // span
+    full, some = bounds[0], bounds[1]
+    scaling = HD ** (-0.5)
+    log_scale = scaling * LOG2E
+    features = q_ref.shape[1] * pl.num_programs(1)
+
+    for g in range(GROUP):
+        part = q_ref[:, g * HD:(g + 1) * HD]
+        q_t[:, g * rows:(g + 1) * rows] = part.T
+        stack[g * rows:(g + 1) * rows, :] = part
+
+    @pl.when(phase == 0)
+    def _():
+        @pl.when(head == 0)
+        def _():
+            dots[...] = jnp.zeros_like(dots)
+
+        def folded(found):
+            return jnp.max(found.reshape(span // 8, 8, wide), axis=0)
+
+        def plain(c, top):
+            found = dot_nn(k_ref[pl.ds(c * span, span), :], q_t[...])
+            scores[c] = found
+            return jnp.maximum(top, folded(found))
+
+        def masked(c, top):
+            found = dot_nn(k_ref[pl.ds(c * span, span), :], q_t[...])
+            place = c * span + lax.broadcasted_iota(jnp.int32, (span, wide), 0)
+            found = jnp.where(place <= limit_ref[...], found, neg_big)
+            scores[c] = found
+            return jnp.maximum(top, folded(found))
+
+        top = jnp.full((8, wide), neg_big, jnp.float32)
+        top = lax.fori_loop(0, full, plain, top)
+        top = lax.fori_loop(full, some, masked, top)
+        top = jnp.max(top, axis=0, keepdims=True) * log_scale
+        total[...] = jnp.zeros_like(total)
+        ones = jnp.ones((16, span), jnp.bfloat16)
+
+        def weigh(c, carry):
+            at = pl.ds(c * span, span)
+            found = jnp.exp2(scores[c] * log_scale - top).astype(jnp.bfloat16)
+            weights[head, at, :] = found
+            values = jnp.concatenate([v_ref[at, :].T, ones], axis=0)
+            total[...] += dot_nn(values, found)
+            return carry
+
+        lax.fori_loop(0, some, weigh, 0)
+        inverse = 1.0 / total[HD:HD + 1, :]
+        recip[head] = jnp.broadcast_to(inverse, (8, wide))
+        out = total[:HD, :] * inverse
+        outs[head] = out
+        square, cross = dots[0], dots[1]
+        for g in range(GROUP):
+            part = out[:, g * rows:(g + 1) * rows].T
+            scaled = g_ref[:, g * HD:(g + 1) * HD].astype(jnp.float32) * gain_ref[:, g * HD:(g + 1) * HD]
+            square = square + part * part
+            cross = cross + scaled * part
+        dots[0], dots[1] = square, cross
+
+    @pl.when(phase == 1)
+    def _():
+        square = jnp.sum(dots[0], axis=-1, keepdims=True) / features
+        center = jnp.sum(dots[1], axis=-1, keepdims=True) / features
+        inverse = lax.rsqrt(square + eps_norm)
+        pull = inverse * inverse * center
+        row_dot = []
+        for g in range(GROUP):
+            cols, lanes = slice(g * HD, (g + 1) * HD), slice(g * rows, (g + 1) * rows)
+            part_t = outs[head, :, lanes]
+            part = part_t.T
+            gain = gain_ref[:, cols]
+            normed_ref[:, cols] = (part * inverse * gain).astype(jnp.bfloat16)
+            scaled = g_ref[:, cols].astype(jnp.float32) * gain
+            grad = inverse * (scaled - part * pull)
+            turned = (grad.T * recip[head, 0:1, lanes]).astype(jnp.bfloat16)
+            grad_t[:, lanes] = turned
+            row_dot.append(jnp.sum(turned.astype(jnp.float32) * part_t, axis=0, keepdims=True))
+        row_dot = jnp.concatenate(row_dot, axis=1)
+        total[...] = jnp.zeros_like(total)
+
+        def back(c, carry):
+            at = pl.ds(c * span, span)
+            chances = weights[head, at, :]
+            dv_ref[at, :] = dot_nt(chances, grad_t[...]).astype(jnp.bfloat16)
+            moved = dot_nn(v_ref[at, :], grad_t[...]) - row_dot
+            moved = (chances.astype(jnp.float32) * moved).astype(jnp.bfloat16)
+            dk_ref[at, :] = (dot_nn(moved, stack[...]) * scaling).astype(jnp.bfloat16)
+            total[:HD, :] += dot_nn(k_ref[at, :].T, moved)
+            return carry
+
+        lax.fori_loop(0, some, back, 0)
+
+        def empty(c, carry):
+            at = pl.ds(c * span, span)
+            dk_ref[at, :] = jnp.zeros((span, HD), jnp.bfloat16)
+            dv_ref[at, :] = jnp.zeros((span, HD), jnp.bfloat16)
+            return carry
+
+        lax.fori_loop(some, blocks, empty, 0)
+        for g in range(GROUP):
+            part = total[:HD, g * rows:(g + 1) * rows].T * scaling
+            dq_ref[:, g * HD:(g + 1) * HD] = part.astype(jnp.bfloat16)
+
+
+def run_layer_kernel(queries, kv, gain, cotangent, limit, bounds):
+    rows = queries.shape[0]
+    seq_len, heads = kv.shape[0], kv.shape[1] // (2 * HD)
+    span = min(SPAN, seq_len)
+    wide = GROUP * rows
+    by_head = lambda p, h, b: (0, h)
+    second = lambda p, h, b: (0, p * h)
+    spec = pl.BlockSpec
+    return pl.pallas_call(
+        layer_kernel,
+        grid_spec=pltpu.PrefetchScalarGridSpec(
+            num_scalar_prefetch=1,
+            grid=(2, heads),
+            in_specs=[
+                spec((rows, GROUP * HD), by_head),
+                spec((seq_len, HD), by_head),
+                spec((seq_len, HD), lambda p, h, b: (0, heads + h)),
+                spec((rows, GROUP * HD), by_head),
+                spec((1, GROUP * HD), by_head),
+                spec((1, wide), lambda p, h, b: (0, 0)),
+            ],
+            out_specs=[
+                spec((rows, GROUP * HD), second),
+                spec((rows, GROUP * HD), second),
+                spec((seq_len, HD), second),
+                spec((seq_len, HD), second),
+            ],
+            scratch_shapes=[
+                pltpu.VMEM((heads, seq_len, wide), jnp.bfloat16),
+                pltpu.VMEM((seq_len // span, span, wide), jnp.float32),
+                pltpu.VMEM((heads, HD, wide), jnp.float32),
+                pltpu.VMEM((heads, 8, wide), jnp.float32),
+                pltpu.VMEM((HD, wide), jnp.bfloat16),
+                pltpu.VMEM((wide, HD), jnp.bfloat16),
+                pltpu.VMEM((HD, wide), jnp.bfloat16),
+                pltpu.VMEM((HD + 16, wide), jnp.float32),
+                pltpu.VMEM((2, rows, HD), jnp.float32),
+            ],
+        ),
+        out_shape=[
+            jax.ShapeDtypeStruct(queries.shape, jnp.bfloat16),
+            jax.ShapeDtypeStruct(queries.shape, jnp.bfloat16),
+            jax.ShapeDtypeStruct((seq_len, heads * HD), jnp.bfloat16),
+            jax.ShapeDtypeStruct((seq_len, heads * HD), jnp.bfloat16),
+        ],
+        compiler_params=pltpu.CompilerParams(vmem_limit_bytes=56 * 1024 * 1024),
+        cost_estimate=pl.CostEstimate(
+            flops=12 * wide * seq_len * HD * heads,
+            bytes_accessed=32 * 1024 * 1024,
+            transcendentals=wide * seq_len * heads,
+        ),
+    )(bounds, queries, kv, kv, cotangent, gain, limit)
+
+
+def on_device_kernel(query_heads, keys_values, grad_output, norm_gain, turn_ids):
+    rows = turn_ids.shape[0]
+    first = lax.axis_index("ctx") * rows
+    own = keys_values[0].reshape(rows, -1)
+    key_turns = lax.all_gather(turn_ids, "ctx", axis=0, tiled=True)
+    earlier = passed_along(own, "section", 1)
+    own_full = lax.all_gather(own, "ctx", axis=0, tiled=True)
+    earlier_full = lax.all_gather(earlier, "ctx", axis=0, tiled=True)
+    limit = jnp.sum((key_turns[None, :] <= turn_ids[:, None]).astype(jnp.int32), axis=1) - 1
+    span = min(SPAN, key_turns.shape[0])
+    bounds = jnp.stack([(first + 1) // span, jnp.max(limit) // span + 1]).astype(jnp.int32)
+    limit = jnp.tile(limit, GROUP)[None, :]
+    results = [
+        run_layer_kernel(
+            query_heads[0, p], full, norm_gain[0, p][None, :], grad_output[0, p], limit, bounds
+        )
+        for p, full in enumerate((own_full, earlier_full))
+    ]
+    sums = [
+        lax.psum_scatter(
+            jnp.concatenate([r[2], r[3]], axis=1), "ctx", scatter_dimension=0, tiled=True
+        )
+        for r in results
+    ]
+    kv_grad = sums[0].astype(jnp.float32) + passed_along(sums[1], "section", -1).astype(jnp.float32)
+    normed = jnp.stack([results[0][0], results[1][0]])[None]
+    grad_q = jnp.stack([results[0][1], results[1][1]])[None]
+    return (normed, grad_q, kv_grad.reshape(keys_values.shape))
+
+
 def solution(mesh):
     in_specs = (
         P("section", None, "ctx", "tp"),
@@ -187,6 +398,7 @@
         P("section", None, "ctx", "tp"),
         P("section", "ctx", None, "tp"),
     )
+    body = on_device_kernel if mesh.shape["tp"] == 1 else on_device
     return jax.shard_map(
-        on_device, mesh=mesh, in_specs=in_specs, out_specs=out_specs, check_vma=False
-    )
+        body, mesh=mesh, in_specs=in_specs, out_specs=out_specs, check_vma=False
+    )

time: 925 us -> 405 us (0.44)
  matrix products: 314 us -> 0 us
  local copies, waits for them, and re-layouts: 151 us -> 13.1 us
  waiting for transfers between devices: 333 us -> 261 us
  Pallas kernels: 0 us -> 59.3 us
  other arithmetic: 67.9 us -> 26.7 us
  loops' own time: 12.5 us -> 0 us
    dot_general x56 -> x0, matrix products: 314 us -> none  [the longest x8 81.6 us: forward_step(): jnp.einsum('hgqk,khd->qhgd', weights.astype(jnp.bfloat16), value_rows, pr...]
    unnamed x4, waiting for transfers between devices: 290 us -> 0.73 us
    reduce_scatter x0 -> x2, waiting for transfers between devices: none -> 170 us  [on_device_kernel(): lax.psum_scatter(jnp.concatenate([r[2], r[3]], axis=1), 'ctx', scatter_di...]
    pallas_call x0 -> x2, Pallas kernels: none -> 59.3 us  [run_layer_kernel(): pl.pallas_call(layer_kernel, grid_spec=pltpu.PrefetchScalarGridSpec(num_s...]
    convert_element_type x4 -> x0, local copies, waits for them, and re-layouts: 50.5 us -> none  [the longest x2 25.8 us: on_device(): producer[2].astype(jnp.bfloat16)]
    slice x19 -> x0, local copies, waits for them, and re-layouts: 46.6 us -> none  [the longest x16 40.6 us: block_terms(): value_rows = kv_rows[:, 1].reshape(row_count, head_count, HD)]
    all_gather x2, waiting for transfers between devices: 35.1 us -> 78.6 us  [the longest x1 41.1 us: on_device_kernel(): earlier_full = lax.all_gather(earlier, 'ctx', axis=0, tiled=True)]
    reduce_sum x12 -> x1, other arithmetic: 34.8 us -> 0.9 us  [on_device_kernel(): jnp.sum((key_turns[None, :] <= turn_ids[:, None]).astype(jnp.int32), axis=1)]
  transfers between devices with their start and end apart: 5 -> 6, of which waited for: 3 -> 5; matrix products, arithmetic and copies ran while one was open for 31% -> 8% of each run, Pallas kernels for 0% -> 15%
where the time goes in v1:
time: 405 us; the launch traced here: 404 us
  waiting for transfers between devices  261 us (64%)
  Pallas kernels  59.3 us (15%)
  other arithmetic  26.7 us (7%)
  blocking collectives  22 us (5%)
  between operations  16.4 us (4%)
  local copies, waits for them, and re-layouts  13.1 us (3%)
  starting transfers between devices  4.67 us (1%)
    reduce_scatter x2, waiting for transfers between devices, on_device_kernel(): lax.psum_scatter(jnp.concatenate([r[2], r[3]], axis=1), 'ctx', scatter_di...  170 us
    pallas_call x2, Pallas kernels, run_layer_kernel(): pl.pallas_call(layer_kernel, grid_spec=pltpu.PrefetchScalarGridSpec(num_s...  59.3 us
    all_gather x1, waiting for transfers between devices, on_device_kernel(): earlier_full = lax.all_gather(earlier, 'ctx', axis=0, tiled=True)  41.1 us
    all_gather x1, waiting for transfers between devices, on_device_kernel(): own_full = lax.all_gather(own, 'ctx', axis=0, tiled=True)  37.5 us
    all_gather x1, blocking collectives, on_device_kernel(): key_turns = lax.all_gather(turn_ids, 'ctx', axis=0, tiled=True)  22 us
    concatenate x2, other arithmetic, on_device_kernel(): jnp.concatenate([r[2], r[3]], axis=1)  16.6 us
    ppermute x2, waiting for transfers between devices, passed_along(): return lax.ppermute(block, axis, route)  11.9 us
  transfers between devices with their start and end apart: 6, of which 5 were waited for; matrix products, arithmetic and copies ran while one was open for 8% of the time, Pallas kernels for 15%

profile of v1, /device:TPU:0, one launch (start us, length us, event | category | flops | bytes accessed | tf_op | source)
XLA Modules:
  0.0 403.7 jit_solution(15043803568289126252)
XLA Ops:
  7.2 1.2 copy.8
  8.4 3.0 collective-permute-start
  11.4 11.9 %collective-permute-done = bf16[128,2048]{1,0:T(8,128)(2,1)S(1)} collective-permute-done((bf16[128,2048]{1,0:T(8,128)(2,1)S(1)}, bf16[128,2048]{1,0:T(8,128)(2,1)S(1)}, u32[]{:S(2)}, u32[]{:S(2)}) %collective-permute-start) | collective-permute-done | bytes 524320 | tf_op jit(solution)/shard_map/ppermute | solution.py:30
  23.3 0.8 copy-done.3
  24.2 0.7 all-gather.4.cloned.1.call-update
  25.0 22.0 %all-gather = s32[16,1,128]{2,1,0:T(1,128)S(1)} all-gather(s32[1,1,128]{2,1,0:T(1,128)} %bitcast.43), channel_id=1, replica_groups=mesh['section'=2,'ctx'=16,'tp'=1] {'ctx'}, dimensions={0}, use_global_device_ids=true | all-gather | bytes 8704 | tf_op jit(solution)/shard_map/all_gather | solution.py:362
  47.0 0.9 convert_reduce_fusion
  47.9 0.6 broadcast_add_fusion
  52.3 1.5 slice_bitcast_fusion.5
  53.8 5.8 %slice_bitcast_fusion.2 = (bf16[128,6144]{1,0:T(8,128)(2,1)}, bf16[128,6144]{1,0:T(8,128)(2,1)}, bf16[128,6144]{1,0:T(8,128)(2,1)}, bf16[128,6144]{1,0:T(8,128)(2,1)}) fusion(bf16[1,2,128,6144]{3,2,1,0:T(8,128)(2,1)} %param.7, bf16[1,2,128,6144]{3,2,1,0:T(8,128)(2,1)} %param.5), kind=kLoop, calls=%fused_computation.6 | loop fusion | bytes 12582912 | tf_op jit(solution)/shard_map/squeeze | solution.py:372
  59.6 41.1 %all-gather.6.cloned.1.call-done.k_ref.v_ref = bf16[2048,2048]{1,0:T(8,128)(2,1)} async-done(((bf16[128,2048]{1,0:T(8,128)(2,1)}), bf16[2048,2048]{1,0:T(8,128)(2,1)}) %all-gather.6.cloned.1.call-update) | async-done | bytes 8388624 | tf_op jit(solution)/shard_map/all_gather | solution.py:365
  100.7 29.6 %shard_map.77 = (bf16[128,6144]{1,0:T(8,128)(2,1)}, bf16[128,6144]{1,0:T(8,128)(2,1)}, bf16[2048,1024]{1,0:T(8,128)(2,1)}, bf16[2048,1024]{1,0:T(8,128)(2,1)}) custom-call(s32[2]{0:T(128)} %pad_add_fusion.bounds, bf16[128,6144]{1,0:T(8,128)(2,1)} %get-tuple-element.27.q_ref, bf16[2048,2048]{1,0:T(8,128)(2,1)} %all-gather.6.cloned.1.call-done.k_ref.v_ref, ...), custom_call_target="tpu_custom_call" | custom-call | flops 19327352832 | bytes 33554432 | tf_op jit(solution)/shard_map/pallas_call | solution.py:312
  130.3 8.2 %pad_maximum_fusion.1 = bf16[2048,2048]{1,0:T(8,128)(2,1)} fusion(bf16[2048,1024]{1,0:T(8,128)(2,1)} %get-tuple-element.18, bf16[2048,1024]{1,0:T(8,128)(2,1)} %get-tuple-element.17), kind=kLoop, calls=%fused_computation.1 | loop fusion | flops 16777216 | bytes 16777216 | tf_op jit(solution)/shard_map/concatenate | solution.py:378
  138.5 37.5 %all-gather.4.cloned.1.call-done.k_ref.v_ref = bf16[2048,2048]{1,0:T(8,128)(2,1)} async-done(((bf16[128,2048]{1,0:T(8,128)(2,1)}), bf16[2048,2048]{1,0:T(8,128)(2,1)}) %all-gather.4.cloned.1.call-update) | async-done | bytes 8388624 | tf_op jit(solution)/shard_map/all_gather | solution.py:364
  176.1 29.7 %shard_map.76 = (bf16[128,6144]{1,0:T(8,128)(2,1)}, bf16[128,6144]{1,0:T(8,128)(2,1)}, bf16[2048,1024]{1,0:T(8,128)(2,1)}, bf16[2048,1024]{1,0:T(8,128)(2,1)}) custom-call(s32[2]{0:T(128)} %pad_add_fusion.bounds, bf16[128,6144]{1,0:T(8,128)(2,1)} %get-tuple-element.28.q_ref, bf16[2048,2048]{1,0:T(8,128)(2,1)} %all-gather.4.cloned.1.call-done.k_ref.v_ref, ...), custom_call_target="tpu_custom_call" | custom-call | flops 19327352832 | bytes 33554432 | tf_op jit(solution)/shard_map/pallas_call | solution.py:312
  205.8 8.5 %pad_maximum_fusion = bf16[2048,2048]{1,0:T(8,128)(2,1)} fusion(bf16[2048,1024]{1,0:T(8,128)(2,1)} %get-tuple-element.16, bf16[2048,1024]{1,0:T(8,128)(2,1)} %get-tuple-element.15), kind=kLoop, calls=%fused_computation | loop fusion | flops 16777216 | bytes 16777216 | tf_op jit(solution)/shard_map/concatenate | solution.py:378
  214.3 1.4 copy-done.2
  215.6 3.5 maximum_bitcast_fusion.1
  219.1 66.7 %reduce-scatter.5.cloned.1.call-done = bf16[128,2048]{1,0:T(8,128)(2,1)} async-done(((bf16[2048,2048]{1,0:T(8,128)(2,1)}), bf16[128,2048]{1,0:T(8,128)(2,1)}) %reduce-scatter.5.cloned.1.call-update) | async-done | bytes 524304 | tf_op jit(solution)/shard_map/reduce_scatter | solution.py:377
  285.9 1.5 collective-permute-start.1
  287.3 3.4 maximum_bitcast_fusion
  290.7 103.5 %reduce-scatter.3.cloned.1.call-done = bf16[128,2048]{1,0:T(8,128)(2,1)} async-done(((bf16[2048,2048]{1,0:T(8,128)(2,1)}), bf16[128,2048]{1,0:T(8,128)(2,1)}) %reduce-scatter.3.cloned.1.call-update) | async-done | bytes 524304 | tf_op jit(solution)/shard_map/reduce_scatter | solution.py:377
  394.2 1.2 convert_add_fusion
  395.3 1.9 reshape.14
  (17 shorter events, 1.4 us)
Async XLA Ops:
  7.2 93.5 %all-gather.6.cloned.1.call-start = ((), (), s32[]{:S(2)}) async-start(), calls=%async_computation.3 | async-start | bytes 8912896 | tf_op jit(solution)/shard_map/all_gather | solution.py:365
  8.4 15.8 %copy-start = (bf16[16,8,2,1024]{3,1,2,0:T(8,128)(2,1)}, bf16[16,8,2,1024]{3,1,2,0:T(8,128)(2,1)S(1)}, u32[]{:S(2)}) copy-start(bf16[16,8,2,1024]{3,1,2,0:T(8,128)(2,1)S(1)} %copy.8) | copy-start | bytes 1572868
  8.4 15.0 %collective-permute-start = (bf16[128,2048]{1,0:T(8,128)(2,1)S(1)}, bf16[128,2048]{1,0:T(8,128)(2,1)S(1)}, u32[]{:S(2)}, u32[]{:S(2)}) collective-permute-start(bf16[128,2048]{1,0:T(8,128)(2,1)S(1)} %bitcast.33), channel_id=1, source_target_pairs={{16,0},{0,16},{17,1},{1,17},{18,2},{2,18},{19,3},{3,19},{20,4},{4,... | collective-permute-start | bytes 1572872 | tf_op jit(solution)/shard_map/ppermute | solution.py:30
  23.3 0.8 copy-start.3
  24.2 151.9 %all-gather.4.cloned.1.call-start = ((), (), s32[]{:S(2)}) async-start(), calls=%async_computation.2 | async-start | bytes 8912896 | tf_op jit(solution)/shard_map/all_gather | solution.py:364
  24.9 260.9 %reduce-scatter.5.cloned.1.call-start = ((), (), s32[]{:S(2)}) async-start(), calls=%async_computation.5 | async-start | bytes 8912896 | tf_op jit(solution)/shard_map/reduce_scatter | solution.py:377
  138.5 255.7 %reduce-scatter.3.cloned.1.call-start = ((), (), s32[]{:S(2)}) async-start(), calls=%async_computation.4 | async-start | bytes 8912896 | tf_op jit(solution)/shard_map/reduce_scatter | solution.py:377
  214.2 1.4 copy-start.2
  215.6 71.7 %copy-start.1 = (bf16[128,6144]{1,0:T(8,128)(2,1)S(1)}, bf16[128,6144]{1,0:T(8,128)(2,1)}, u32[]{:S(2)}) copy-start(bf16[128,6144]{1,0:T(8,128)(2,1)} %get-tuple-element.12) | copy-start | bytes 4718596
  285.9 108.3 %collective-permute-start.1 = (bf16[128,2048]{1,0:T(8,128)(2,1)}, bf16[128,2048]{1,0:T(8,128)(2,1)S(1)}, u32[]{:S(2)}, u32[]{:S(2)}) collective-permute-start(bf16[128,2048]{1,0:T(8,128)(2,1)} %reduce-scatter.5.cloned.1.call-done), channel_id=1, source_target_pairs={{16,0},{0,16},{17,1},{1,17},{18,2},{2,18},{19,3},{3,19},{20,4},{4,... | collective-permute-start | bytes 1572872 | tf_op jit(solution)/shard_map/ppermute | solution.py:30
Sparse Core Ops, SparseCore 0:
  24.3 76.3 all-gather.5
  102.8 73.1 all-gather.3
  180.1 105.6 reduce-scatter.4
  289.8 104.3 reduce-scatter.2

commit v2 on v1

--- a/solution.py
+++ b/solution.py
@@ -187,17 +187,19 @@
 
 
 def layer_kernel(
-    bounds, q_ref, k_ref, v_ref, g_ref, gain_ref, limit_ref,
-    normed_ref, dq_ref, dk_ref, dv_ref,
+    bounds, q_ref, mine_ref, other_ref, g_ref, gain_ref, limit_ref,
+    normed_ref, dq_ref, keep_ref, send_ref,
     weights, scores, outs, recip, q_t, stack, grad_t, total, dots,
 ):
     phase, head = pl.program_id(0), pl.program_id(1)
-    seq_len = k_ref.shape[0]
+    half = mine_ref.shape[0]
+    key_cols, value_cols = slice(0, HD), slice(HD, 2 * HD)
     rows = q_ref.shape[0]
     wide = GROUP * rows
     span = scores.shape[1]
-    blocks = seq_len // span
-    full, some = bounds[0], bounds[1]
+    blocks = half // span
+    side = bounds[4]
+    sides = ((mine_ref, keep_ref, side, 0), (other_ref, send_ref, 1 - side, 1))
     scaling = HD ** (-0.5)
     log_scale = scaling * LOG2E
     features = q_ref.shape[1] * pl.num_programs(1)
@@ -216,34 +218,39 @@
         def folded(found):
             return jnp.max(found.reshape(span // 8, 8, wide), axis=0)
 
-        def plain(c, top):
-            found = dot_nn(k_ref[pl.ds(c * span, span), :], q_t[...])
-            scores[c] = found
-            return jnp.maximum(top, folded(found))
-
-        def masked(c, top):
-            found = dot_nn(k_ref[pl.ds(c * span, span), :], q_t[...])
-            place = c * span + lax.broadcasted_iota(jnp.int32, (span, wide), 0)
-            found = jnp.where(place <= limit_ref[...], found, neg_big)
-            scores[c] = found
-            return jnp.maximum(top, folded(found))
-
         top = jnp.full((8, wide), neg_big, jnp.float32)
-        top = lax.fori_loop(0, full, plain, top)
-        top = lax.fori_loop(full, some, masked, top)
+        for kv_ref, _, parity, u in sides:
+            def found_at(c):
+                return dot_nn(kv_ref[pl.ds(c * span, span), key_cols], q_t[...])
+
+            def plain(c, top):
+                found = found_at(c)
+                scores[u * blocks + c] = found
+                return jnp.maximum(top, folded(found))
+
+            def masked(c, top):
+                line = lax.broadcasted_iota(jnp.int32, (rows, wide), 0)
+                place = jnp.concatenate([line + 2 * rows * k for k in range(span // rows)], axis=0)
+                start = 2 * c * span + parity * rows
+                found = jnp.where(place <= limit_ref[...] - start, found_at(c), neg_big)
+                scores[u * blocks + c] = found
+                return jnp.maximum(top, folded(found))
+
+            top = lax.fori_loop(0, bounds[2 * u], plain, top)
+            top = lax.fori_loop(bounds[2 * u], bounds[2 * u + 1], masked, top)
         top = jnp.max(top, axis=0, keepdims=True) * log_scale
         total[...] = jnp.zeros_like(total)
         ones = jnp.ones((16, span), jnp.bfloat16)
 
-        def weigh(c, carry):
-            at = pl.ds(c * span, span)
-            found = jnp.exp2(scores[c] * log_scale - top).astype(jnp.bfloat16)
-            weights[head, at, :] = found
-            values = jnp.concatenate([v_ref[at, :].T, ones], axis=0)
-            total[...] += dot_nn(values, found)
-            return carry
-
-        lax.fori_loop(0, some, weigh, 0)
+        for kv_ref, _, _, u in sides:
+            def weigh(c, carry):
+                found = jnp.exp2(scores[u * blocks + c] * log_scale - top).astype(jnp.bfloat16)
+                weights[head, u * blocks + c] = found
+                values = jnp.concatenate([kv_ref[pl.ds(c * span, span), value_cols].T, ones], axis=0)
+                total[...] += dot_nn(values, found)
+                return carry
+
+            lax.fori_loop(0, bounds[2 * u + 1], weigh, 0)
         inverse = 1.0 / total[HD:HD + 1, :]
         recip[head] = jnp.broadcast_to(inverse, (8, wide))
         out = total[:HD, :] * inverse
@@ -277,59 +284,59 @@
         row_dot = jnp.concatenate(row_dot, axis=1)
         total[...] = jnp.zeros_like(total)
 
-        def back(c, carry):
-            at = pl.ds(c * span, span)
-            chances = weights[head, at, :]
-            dv_ref[at, :] = dot_nt(chances, grad_t[...]).astype(jnp.bfloat16)
-            moved = dot_nn(v_ref[at, :], grad_t[...]) - row_dot
-            moved = (chances.astype(jnp.float32) * moved).astype(jnp.bfloat16)
-            dk_ref[at, :] = (dot_nn(moved, stack[...]) * scaling).astype(jnp.bfloat16)
-            total[:HD, :] += dot_nn(k_ref[at, :].T, moved)
-            return carry
-
-        lax.fori_loop(0, some, back, 0)
-
-        def empty(c, carry):
-            at = pl.ds(c * span, span)
-            dk_ref[at, :] = jnp.zeros((span, HD), jnp.bfloat16)
-            dv_ref[at, :] = jnp.zeros((span, HD), jnp.bfloat16)
-            return carry
-
-        lax.fori_loop(some, blocks, empty, 0)
+        for kv_ref, grad_ref, _, u in sides:
+            def back(c, carry):
+                at = pl.ds(c * span, span)
+                chances = weights[head, u * blocks + c]
+                grad_ref[at, value_cols] = dot_nt(chances, grad_t[...]).astype(jnp.bfloat16)
+                moved = dot_nn(kv_ref[at, value_cols], grad_t[...]) - row_dot
+                moved = (chances.astype(jnp.float32) * moved).astype(jnp.bfloat16)
+                grad_ref[at, key_cols] = (dot_nn(moved, stack[...]) * scaling).astype(jnp.bfloat16)
+                total[:HD, :] += dot_nn(kv_ref[at, key_cols].T, moved)
+                return carry
+
+            def empty(c, carry):
+                grad_ref[pl.ds(c * span, span), :] = jnp.zeros((span, 2 * HD), jnp.bfloat16)
+                return carry
+
+            lax.fori_loop(0, bounds[2 * u + 1], back, 0)
+            lax.fori_loop(bounds[2 * u + 1], blocks, empty, 0)
         for g in range(GROUP):
             part = total[:HD, g * rows:(g + 1) * rows].T * scaling
             dq_ref[:, g * HD:(g + 1) * HD] = part.astype(jnp.bfloat16)
 
 
-def run_layer_kernel(queries, kv, gain, cotangent, limit, bounds):
-    rows = queries.shape[0]
-    seq_len, heads = kv.shape[0], kv.shape[1] // (2 * HD)
-    span = min(SPAN, seq_len)
+def run_layer_kernel(layer, queries, mine, other, gain, cotangent, limit, bounds, span):
+    rows = queries.shape[2]
+    half, heads = mine.shape[0], mine.shape[1] // (2 * HD)
+    seq_len = 2 * half
     wide = GROUP * rows
+    whole = lambda p, h, b: (0, layer, 0, h)
     by_head = lambda p, h, b: (0, h)
     second = lambda p, h, b: (0, p * h)
     spec = pl.BlockSpec
+    flat = (rows, queries.shape[3])
     return pl.pallas_call(
         layer_kernel,
         grid_spec=pltpu.PrefetchScalarGridSpec(
             num_scalar_prefetch=1,
             grid=(2, heads),
             in_specs=[
-                spec((rows, GROUP * HD), by_head),
-                spec((seq_len, HD), by_head),
-                spec((seq_len, HD), lambda p, h, b: (0, heads + h)),
-                spec((rows, GROUP * HD), by_head),
+                spec((None, None, rows, GROUP * HD), whole),
+                spec((half, 2 * HD), by_head),
+                spec((half, 2 * HD), by_head),
+                spec((None, None, rows, GROUP * HD), whole),
                 spec((1, GROUP * HD), by_head),
                 spec((1, wide), lambda p, h, b: (0, 0)),
             ],
             out_specs=[
                 spec((rows, GROUP * HD), second),
                 spec((rows, GROUP * HD), second),
-                spec((seq_len, HD), second),
-                spec((seq_len, HD), second),
+                spec((half, 2 * HD), second),
+                spec((half, 2 * HD), second),
             ],
             scratch_shapes=[
-                pltpu.VMEM((heads, seq_len, wide), jnp.bfloat16),
+                pltpu.VMEM((heads, seq_len // span, span, wide), jnp.bfloat16),
                 pltpu.VMEM((seq_len // span, span, wide), jnp.float32),
                 pltpu.VMEM((heads, HD, wide), jnp.float32),
                 pltpu.VMEM((heads, 8, wide), jnp.float32),
@@ -341,10 +348,10 @@
             ],
         ),
         out_shape=[
-            jax.ShapeDtypeStruct(queries.shape, jnp.bfloat16),
-            jax.ShapeDtypeStruct(queries.shape, jnp.bfloat16),
-            jax.ShapeDtypeStruct((seq_len, heads * HD), jnp.bfloat16),
-            jax.ShapeDtypeStruct((seq_len, heads * HD), jnp.bfloat16),
+            jax.ShapeDtypeStruct(flat, jnp.bfloat16),
+            jax.ShapeDtypeStruct(flat, jnp.bfloat16),
+            jax.ShapeDtypeStruct(mine.shape, jnp.bfloat16),
+            jax.ShapeDtypeStruct(mine.shape, jnp.bfloat16),
         ],
         compiler_params=pltpu.CompilerParams(vmem_limit_bytes=56 * 1024 * 1024),
         cost_estimate=pl.CostEstimate(
@@ -352,34 +359,55 @@
             bytes_accessed=32 * 1024 * 1024,
             transcendentals=wide * seq_len * heads,
         ),
-    )(bounds, queries, kv, kv, cotangent, gain, limit)
+    )(bounds, queries, mine, other, cotangent, gain, limit)
 
 
 def on_device_kernel(query_heads, keys_values, grad_output, norm_gain, turn_ids):
     rows = turn_ids.shape[0]
-    first = lax.axis_index("ctx") * rows
-    own = keys_values[0].reshape(rows, -1)
-    key_turns = lax.all_gather(turn_ids, "ctx", axis=0, tiled=True)
+    width = lax.axis_size("ctx")
+    here = lax.axis_index("ctx")
+    side = lax.rem(here, 2)
+    first = here * rows
+    teams = [list(range(start, width, 2)) for start in range(2)]
+    pairs = [(i, i + 1 - 2 * (i % 2)) for i in range(width)]
+    heads = keys_values.shape[3] // HD
+    own = keys_values.reshape(rows, 2, heads, HD).transpose(0, 2, 1, 3).reshape(rows, -1)
+
+    def gathered(block):
+        mine = lax.all_gather(block, "ctx", axis=0, tiled=True, axis_index_groups=teams)
+        return (mine, lax.ppermute(mine, "ctx", pairs))
+
+    def spread(keep, send):
+        came = lax.ppermute(send, "ctx", pairs)
+        both = (keep.astype(jnp.float32) + came.astype(jnp.float32)).astype(jnp.bfloat16)
+        return lax.psum_scatter(
+            both, "ctx", scatter_dimension=0, tiled=True, axis_index_groups=teams
+        )
+
+    later = jnp.where(here + 1 < width, passed_along(turn_ids, "ctx", -1), -1)
     earlier = passed_along(own, "section", 1)
-    own_full = lax.all_gather(own, "ctx", axis=0, tiled=True)
-    earlier_full = lax.all_gather(earlier, "ctx", axis=0, tiled=True)
-    limit = jnp.sum((key_turns[None, :] <= turn_ids[:, None]).astype(jnp.int32), axis=1) - 1
-    span = min(SPAN, key_turns.shape[0])
-    bounds = jnp.stack([(first + 1) // span, jnp.max(limit) // span + 1]).astype(jnp.int32)
+    reach = (turn_ids[None, :] <= turn_ids[:, None]).astype(jnp.int32)
+    reach = reach + (later[None, :] == turn_ids[:, None]).astype(jnp.int32)
+    limit = first + jnp.sum(reach, axis=1) - 1
+    half = rows * width // 2
+    span = SPAN if half % SPAN == 0 and SPAN % rows == 0 else half
+    starts = 2 * span * jnp.arange(half // span, dtype=jnp.int32)
+    bounds = []
+    for parity in (side, 1 - side):
+        lowest = starts + parity * rows
+        highest = lowest + 2 * span - rows - 1
+        bounds += [jnp.sum(highest <= first), jnp.sum(lowest <= jnp.max(limit))]
+    bounds = jnp.stack(bounds + [side]).astype(jnp.int32)
     limit = jnp.tile(limit, GROUP)[None, :]
     results = [
         run_layer_kernel(
-            query_heads[0, p], full, norm_gain[0, p][None, :], grad_output[0, p], limit, bounds
-        )
-        for p, full in enumerate((own_full, earlier_full))
+            p, query_heads, *gathered(block), norm_gain[0, p][None, :], grad_output, limit, bounds, span
+        )
+        for p, block in enumerate((own, earlier))
     ]
-    sums = [
-        lax.psum_scatter(
-            jnp.concatenate([r[2], r[3]], axis=1), "ctx", scatter_dimension=0, tiled=True
-        )
-        for r in results
-    ]
+    sums = [spread(r[2], r[3]) for r in results]
     kv_grad = sums[0].astype(jnp.float32) + passed_along(sums[1], "section", -1).astype(jnp.float32)
+    kv_grad = kv_grad.reshape(rows, heads, 2, HD).transpose(0, 2, 1, 3)
     normed = jnp.stack([results[0][0], results[1][0]])[None]
     grad_q = jnp.stack([results[0][1], results[1][1]])[None]
     return (normed, grad_q, kv_grad.reshape(keys_values.shape))
@@ -398,7 +426,8 @@
         P("section", None, "ctx", "tp"),
         P("section", "ctx", None, "tp"),
     )
-    body = on_device_kernel if mesh.shape["tp"] == 1 else on_device
+    fits = mesh.shape["tp"] == 1 and mesh.shape["ctx"] % 2 == 0
+    body = on_device_kernel if fits else on_device
     return jax.shard_map(
         body, mesh=mesh, in_specs=in_specs, out_specs=out_specs, check_vma=False
     )

time: 405 us -> 390 us (0.963)
  Pallas kernels: 59.3 us -> 88.2 us
  blocking collectives: 22 us -> 0 us
  waiting for transfers between devices: 261 us -> 244 us
    reduce_scatter x2, waiting for transfers between devices: 170 us -> 131 us  [spread(): lax.psum_scatter(both, 'ctx', scatter_dimension=0, tiled=True, axis_index...]
    pallas_call x2, Pallas kernels: 59.3 us -> 88.2 us  [run_layer_kernel(): pl.pallas_call(layer_kernel, grid_spec=pltpu.PrefetchScalarGridSpec(num_s...]
    all_gather x1 -> x0, blocking collectives: 22 us -> none  [on_device_kernel(): key_turns = lax.all_gather(turn_ids, 'ctx', axis=0, tiled=True)]
    concatenate x2 -> x0, other arithmetic: 16.6 us -> none  [on_device_kernel(): jnp.concatenate([r[2], r[3]], axis=1)]
    all_gather x2, waiting for transfers between devices: 78.6 us -> 94.1 us  [gathered(): lax.all_gather(block, 'ctx', axis=0, tiled=True, axis_index_groups=teams)]
    convert_element_type x0 -> x2, other arithmetic: none -> 13.8 us  [spread(): (keep.astype(jnp.float32) + came.astype(jnp.float32)).astype(jnp.bfloat16)]
    ppermute x0 -> x4, waiting for transfers between devices: none -> 7 us  [the longest x2 7 us: spread(): came = lax.ppermute(send, 'ctx', pairs)]
    squeeze x1 -> x0, local copies, waits for them, and re-layouts: 5.76 us -> none  [on_device_kernel(): grad_output[0, p]]
  transfers between devices with their start and end apart: 6 -> 11, of which waited for: 5 -> 6; matrix products, arithmetic and copies ran while one was open for 8% -> 8% of each run, Pallas kernels for 15% -> 23%
where the time goes in v2:
time: 390 us; the launch traced here: 389 us
  waiting for transfers between devices  244 us (63%)
  Pallas kernels  88.2 us (23%)
  other arithmetic  25.2 us (6%)
  between operations  13.8 us (4%)
  local copies, waits for them, and re-layouts  10.7 us (3%)
  starting transfers between devices  7.08 us (2%)
    reduce_scatter x2, waiting for transfers between devices, spread(): lax.psum_scatter(both, 'ctx', scatter_dimension=0, tiled=True, axis_index...  131 us
    all_gather x2, waiting for transfers between devices, gathered(): lax.all_gather(block, 'ctx', axis=0, tiled=True, axis_index_groups=teams)  94.1 us
    pallas_call x2, Pallas kernels, run_layer_kernel(): pl.pallas_call(layer_kernel, grid_spec=pltpu.PrefetchScalarGridSpec(num_s...  88.2 us
    convert_element_type x2, other arithmetic, spread(): (keep.astype(jnp.float32) + came.astype(jnp.float32)).astype(jnp.bfloat16)  13.8 us
    ppermute x3, waiting for transfers between devices, passed_along(): return lax.ppermute(block, axis, route)  11.9 us
  transfers between devices with their start and end apart: 11, of which 6 were waited for; matrix products, arithmetic and copies ran while one was open for 8% of the time, Pallas kernels for 23%

profile of v2, /device:TPU:0, one launch (start us, length us, event | category | flops | bytes accessed | tf_op | source)
XLA Modules:
  0.0 389.3 jit_solution(11194841866696012432)
XLA Ops:
  7.2 1.4 reshape.26
  8.6 3.0 collective-permute-start.2
  11.7 11.9 %collective-permute-done.2 = bf16[128,2048]{1,0:T(8,128)(2,1)S(1)} collective-permute-done((bf16[128,2048]{1,0:T(8,128)(2,1)S(1)}, bf16[128,2048]{1,0:T(8,128)(2,1)S(1)}, u32[]{:S(2)}, u32[]{:S(2)}) %collective-permute-start.2) | collective-permute-done | bytes 524320 | tf_op jit(solution)/shard_map/ppermute | solution.py:30
  23.6 0.8 copy-done.3
  24.5 75.0 %all-gather.5.cloned.1.call-done.mine_ref = bf16[1024,2048]{1,0:T(8,128)(2,1)} async-done(((bf16[128,2048]{1,0:T(8,128)(2,1)}), bf16[1024,2048]{1,0:T(8,128)(2,1)}) %all-gather.5.cloned.1.call-update) | async-done | bytes 4194320 | tf_op jit(solution)/shard_map/all_gather | solution.py:377
  99.5 1.7 collective-permute-start
  101.3 1.5 slice_bitcast_fusion.1
  103.4 0.9 add_reduce_fusion
  105.5 1.3 fusion.1
  106.8 3.2 stack.41.bounds
  110.0 44.2 %shard_map.77 = (bf16[128,6144]{1,0:T(8,128)(2,1)}, bf16[128,6144]{1,0:T(8,128)(2,1)}, bf16[1024,2048]{1,0:T(8,128)(2,1)}, bf16[1024,2048]{1,0:T(8,128)(2,1)}) custom-call(s32[5]{0:T(128)} %stack.41.bounds, bf16[1,2,128,6144]{3,2,1,0:T(8,128)(2,1)} %q_ref.3, bf16[1024,2048]{1,0:T(8,128)(2,1)} %all-gather.5.cloned.1.call-done.mine_ref, ...), custom_call_target="tpu_custom_call" | custom-call | flops 19327352832 | bytes 33554432 | tf_op jit(solution)/shard_map/pallas_call | solution.py:319
  154.2 19.1 %all-gather.3.cloned.1.call-done.mine_ref = bf16[1024,2048]{1,0:T(8,128)(2,1)} async-done(((bf16[128,2048]{1,0:T(8,128)(2,1)}), bf16[1024,2048]{1,0:T(8,128)(2,1)}) %all-gather.3.cloned.1.call-update) | async-done | bytes 4194320 | tf_op jit(solution)/shard_map/all_gather | solution.py:377
  173.3 7.7 %add_convert_fusion = bf16[1024,2048]{1,0:T(8,128)(2,1)} fusion(bf16[1024,2048]{1,0:T(8,128)(2,1)} %collective-permute-done.5, bf16[1024,2048]{1,0:T(8,128)(2,1)} %get-tuple-element.17), kind=kLoop, calls=%fused_computation | loop fusion | flops 8388608 | bytes 12582912 | tf_op jit(solution)/shard_map/convert_element_type | solution.py:382
  181.3 44.0 %shard_map.76 = (bf16[128,6144]{1,0:T(8,128)(2,1)}, bf16[128,6144]{1,0:T(8,128)(2,1)}, bf16[1024,2048]{1,0:T(8,128)(2,1)}, bf16[1024,2048]{1,0:T(8,128)(2,1)}) custom-call(s32[5]{0:T(128)} %stack.41.bounds, bf16[1,2,128,6144]{3,2,1,0:T(8,128)(2,1)} %q_ref.3, bf16[1024,2048]{1,0:T(8,128)(2,1)} %all-gather.3.cloned.1.call-done.mine_ref, ...), custom_call_target="tpu_custom_call" | custom-call | flops 19327352832 | bytes 33554432 | tf_op jit(solution)/shard_map/pallas_call | solution.py:319
  225.8 7.0 %collective-permute-done.4 = bf16[1024,2048]{1,0:T(8,128)(2,1)S(1)} collective-permute-done((bf16[1024,2048]{1,0:T(8,128)(2,1)}, bf16[1024,2048]{1,0:T(8,128)(2,1)S(1)}, u32[]{:S(2)}, u32[]{:S(2)}) %collective-permute-start.4) | collective-permute-done | bytes 4194336 | tf_op jit(solution)/shard_map/ppermute | solution.py:381
  232.8 6.1 %add_convert_fusion.1 = bf16[1024,2048]{1,0:T(8,128)(2,1)} fusion(bf16[1024,2048]{1,0:T(8,128)(2,1)S(1)} %collective-permute-done.4, bf16[1024,2048]{1,0:T(8,128)(2,1)} %get-tuple-element.15), kind=kLoop, calls=%fused_computation.1 | loop fusion | flops 8388608 | bytes 12582912 | tf_op jit(solution)/shard_map/convert_element_type | solution.py:382
  238.9 1.4 copy-done.2
  240.3 3.4 maximum_bitcast_fusion.1
  243.7 44.4 %reduce-scatter.5.cloned.1.call-done = bf16[128,2048]{1,0:T(8,128)(2,1)} async-done(((bf16[1024,2048]{1,0:T(8,128)(2,1)}), bf16[128,2048]{1,0:T(8,128)(2,1)}) %reduce-scatter.5.cloned.1.call-update) | async-done | bytes 524304 | tf_op jit(solution)/shard_map/reduce_scatter | solution.py:383
  288.2 1.5 collective-permute-start.6
  289.6 3.4 maximum_bitcast_fusion
  293.0 86.8 %reduce-scatter.3.cloned.1.call-done = bf16[128,2048]{1,0:T(8,128)(2,1)} async-done(((bf16[1024,2048]{1,0:T(8,128)(2,1)}), bf16[128,2048]{1,0:T(8,128)(2,1)}) %reduce-scatter.3.cloned.1.call-update) | async-done | bytes 524304 | tf_op jit(solution)/shard_map/reduce_scatter | solution.py:383
  379.8 1.2 convert_add_fusion
  380.9 1.9 reshape.27
  (28 shorter events, 2.8 us)
Async XLA Ops:
  7.2 92.3 %all-gather.5.cloned.1.call-start = ((), (), s32[]{:S(2)}) async-start(), calls=%async_computation.3 | async-start | bytes 4718592 | tf_op jit(solution)/shard_map/all_gather | solution.py:377
  8.6 90.8 %copy-start = (bf16[128,2048]{1,0:T(8,128)(2,1)}, bf16[128,2048]{1,0:T(8,128)(2,1)S(1)}, u32[]{:S(2)}) copy-start(bf16[128,2048]{1,0:T(8,128)(2,1)S(1)} %reshape.26) | copy-start | bytes 1572868
  8.6 15.0 %collective-permute-start.2 = (bf16[128,2048]{1,0:T(8,128)(2,1)S(1)}, bf16[128,2048]{1,0:T(8,128)(2,1)S(1)}, u32[]{:S(2)}, u32[]{:S(2)}) collective-permute-start(bf16[128,2048]{1,0:T(8,128)(2,1)S(1)} %reshape.26), channel_id=1, source_target_pairs={{16,0},{0,16},{17,1},{1,17},{18,2},{2,18},{19,3},{3,19},{20,4},{4,... | collective-permute-start | bytes 1572872 | tf_op jit(solution)/shard_map/ppermute | solution.py:30
  23.6 0.8 copy-start.3
  24.4 148.9 %all-gather.3.cloned.1.call-start = ((), (), s32[]{:S(2)}) async-start(), calls=%async_computation.2 | async-start | bytes 4718592 | tf_op jit(solution)/shard_map/all_gather | solution.py:377
  99.4 10.5 %collective-permute-start.3 = (bf16[1024,2048]{1,0:T(8,128)(2,1)}, bf16[1024,2048]{1,0:T(8,128)(2,1)}, u32[]{:S(2)}, u32[]{:S(2)}) collective-permute-start(bf16[1024,2048]{1,0:T(8,128)(2,1)} %all-gather.5.cloned.1.call-done.mine_ref), channel_id=1, source_target_pairs={{0,1},{1,0},{2,3},{3,2},{4,5},{5,4},{6,7},{7,6},{8,9},{9,8},{10,11... | collective-permute-start | bytes 12582920 | tf_op jit(solution)/shard_map/ppermute | solution.py:378
  99.5 188.7 %reduce-scatter.5.cloned.1.call-start = ((), (), s32[]{:S(2)}) async-start(), calls=%async_computation.5 | async-start | bytes 4718592 | tf_op jit(solution)/shard_map/reduce_scatter | solution.py:383
  99.5 3.9 %collective-permute-start = (s32[128]{0:T(128)}, s32[128]{0:T(128)S(1)}, u32[]{:S(2)}, u32[]{:S(2)}) collective-permute-start(s32[128]{0:T(128)} %param.9), channel_id=1, source_target_pairs={{1,0},{2,1},{3,2},{4,3},{5,4},{6,5},{7,6},{8,7},{9,8},{10,9},{11,1... | collective-permute-start | bytes 1544 | tf_op jit(solution)/shard_map/ppermute | solution.py:30
  154.2 19.1 %collective-permute-start.5 = (bf16[1024,2048]{1,0:T(8,128)(2,1)}, bf16[1024,2048]{1,0:T(8,128)(2,1)}, u32[]{:S(2)}, u32[]{:S(2)}) collective-permute-start(bf16[1024,2048]{1,0:T(8,128)(2,1)} %get-tuple-element.18), channel_id=1, source_target_pairs={{0,1},{1,0},{2,3},{3,2},{4,5},{5,4},{6,7},{7,6},{8,9},{9,8},{10,11... | collective-permute-start | bytes 12582920 | tf_op jit(solution)/shard_map/ppermute | solution.py:381
  173.3 8.0 %collective-permute-start.1 = (bf16[1024,2048]{1,0:T(8,128)(2,1)}, bf16[1024,2048]{1,0:T(8,128)(2,1)}, u32[]{:S(2)}, u32[]{:S(2)}) collective-permute-start(bf16[1024,2048]{1,0:T(8,128)(2,1)} %all-gather.3.cloned.1.call-done.mine_ref), channel_id=1, source_target_pairs={{0,1},{1,0},{2,3},{3,2},{4,5},{5,4},{6,7},{7,6},{8,9},{9,8},{10,11... | collective-permute-start | bytes 12582920 | tf_op jit(solution)/shard_map/ppermute | solution.py:378
  181.0 198.7 %reduce-scatter.3.cloned.1.call-start = ((), (), s32[]{:S(2)}) async-start(), calls=%async_computation.4 | async-start | bytes 4718592 | tf_op jit(solution)/shard_map/reduce_scatter | solution.py:383
  225.3 7.5 %collective-permute-start.4 = (bf16[1024,2048]{1,0:T(8,128)(2,1)}, bf16[1024,2048]{1,0:T(8,128)(2,1)S(1)}, u32[]{:S(2)}, u32[]{:S(2)}) collective-permute-start(bf16[1024,2048]{1,0:T(8,128)(2,1)} %get-tuple-element.16), channel_id=1, source_target_pairs={{0,1},{1,0},{2,3},{3,2},{4,5},{5,4},{6,7},{7,6},{8,9},{9,8},{10,11... | collective-permute-start | bytes 12582920 | tf_op jit(solution)/shard_map/ppermute | solution.py:381
  238.9 1.4 copy-start.2
  238.9 50.7 %copy-start.1 = (bf16[128,6144]{1,0:T(8,128)(2,1)S(1)}, bf16[128,6144]{1,0:T(8,128)(2,1)}, u32[]{:S(2)}) copy-start(bf16[128,6144]{1,0:T(8,128)(2,1)} %get-tuple-element.12) | copy-start | bytes 4718596
  288.2 91.6 %collective-permute-start.6 = (bf16[128,2048]{1,0:T(8,128)(2,1)}, bf16[128,2048]{1,0:T(8,128)(2,1)S(1)}, u32[]{:S(2)}, u32[]{:S(2)}) collective-permute-start(bf16[128,2048]{1,0:T(8,128)(2,1)} %reduce-scatter.5.cloned.1.call-done), channel_id=1, source_target_pairs={{16,0},{0,16},{17,1},{1,17},{18,2},{2,18},{19,3},{3,19},{20,4},{4,... | collective-permute-start | bytes 1572872 | tf_op jit(solution)/shard_map/ppermute | solution.py:30
Sparse Core Ops, SparseCore 0:
  24.5 74.8 all-gather.4
  101.6 71.6 all-gather.2
  181.2 106.9 reduce-scatter.4
  292.1 87.6 reduce-scatter.2
